TPU v7x, 32 devices: a whole 2x2x4 slice. The times are simulated.
32 devices in a mesh: dp: 4 (over y, x), seq: 8 (over z, core).
Axes of the slice: x: 2, y: 2, z: 4, core: 2. Of those that a mesh axis runs over, the one named last changes fastest.
Arguments:
- tokens: bfloat16 [8, 1024, 768], P('dp', 'seq'), may hold values from -6 to 6
- query_weight: float32 [768, 768], P(('dp', 'seq')), may hold values from -0.21875 to 0.21875
- query_bias: float32 [768], P(('dp', 'seq')), may hold values from -3 to 3
- key_weight: float32 [768, 768], P(('dp', 'seq')), may hold values from -0.21875 to 0.21875
- value_weight: float32 [768, 768], P(('dp', 'seq')), may hold values from -0.21875 to 0.21875
- value_bias: float32 [768], P(('dp', 'seq')), may hold values from -3 to 3
- out_weight: float32 [768, 768], P(('dp', 'seq')), may hold values from -0.875 to 0.875
- out_bias: float32 [768], P(('dp', 'seq')), may hold values from -3 to 3
- first_gain: float32 [768], P(('dp', 'seq')), may hold values from 0.5 to 1.5
- attention_norm_shift: float32 [768], P(('dp', 'seq')), may hold values from -3 to 3
- expand_weight: float32 [768, 3072], P(('dp', 'seq')), may hold values from -0.21875 to 0.21875
- expand_bias: float32 [3072], P(('dp', 'seq')), may hold values from -3 to 3
- reduce_weight: float32 [3072, 768], P(('dp', 'seq')), may hold values from -0.109375 to 0.109375
- reduce_bias: float32 [768], P(('dp', 'seq')), may hold values from -3 to 3
- second_gain: float32 [768], P(('dp', 'seq')), may hold values from 0.5 to 1.5
- second_shift: float32 [768], P(('dp', 'seq')), may hold values from -3 to 3
- lengths: int32 [8, 64], P('dp'), may hold values from 0 to 896, as said below
- cotangent: bfloat16 [8, 1024, 768], P('dp', 'seq'), may hold values from -6 to 6
Outputs:
- activations: bfloat16 [8, 1024, 768], P('dp', 'seq')
- tokens_gradient: float32 [8, 1024, 768], P('dp', 'seq')
- query_weight_gradient: float32 [768, 768], P(('dp', 'seq'))
- query_bias_gradient: float32 [768], P(('dp', 'seq'))
- key_weight_gradient: float32 [768, 768], P(('dp', 'seq'))
- value_weight_gradient: float32 [768, 768], P(('dp', 'seq'))
- value_bias_gradient: float32 [768], P(('dp', 'seq'))
- out_weight_gradient: float32 [768, 768], P(('dp', 'seq'))
- output_bias_gradient: float32 [768], P(('dp', 'seq'))
- first_gain_gradient: float32 [768], P(('dp', 'seq'))
- first_shift_gradient: float32 [768], P(('dp', 'seq'))
- expand_weight_gradient: float32 [768, 3072], P(('dp', 'seq'))
- expand_bias_gradient: float32 [3072], P(('dp', 'seq'))
- reduce_weight_gradient: float32 [3072, 768], P(('dp', 'seq'))
- reduce_bias_gradient: float32 [768], P(('dp', 'seq'))
- second_gain_gradient: float32 [768], P(('dp', 'seq'))
- second_shift_gradient: float32 [768], P(('dp', 'seq'))
Inputs may be any that keep to these rules, and one draw needn't show every extreme that they name: The 64 lengths of a stream sum to 1024; unused slots are 0. In each group of 2 streams that share an index of dp, one stream has an item of exactly 896 rows that starts within the first 128 rows and ends within the last 128 rows.
All inputs are finite; a program needn't handle non-finite values.
Results may differ from a plain program's by a relative error of at most 0.018.
Values may be sent and summed in bfloat16 or wider, within the bound.
No kernel may reach another device: no remote copies, remote signals or barrier semaphores. Data moves between devices by JAX's collectives and lax.ppermute only.
A program may use at most 192 MiB of HBM per device.

v0:
```python
import jax
import jax.numpy as jnp
from jax import lax
from jax.sharding import PartitionSpec as P

D = 768
HEADS = 12
HD = 64


NEGATIVE = -1e30
EPSILON = 1e-12


def norm_rows(value_rows):
    centre = jnp.mean(value_rows, axis=-1, keepdims=True)
    centred = value_rows - centre
    inverse = lax.rsqrt(jnp.mean(centred * centred, axis=-1, keepdims=True) + EPSILON)
    return (centred * inverse, inverse)


def norm_back(upward, normed, inverse):
    mean_up = jnp.mean(upward, axis=-1, keepdims=True)
    mean_cross = jnp.mean(upward * normed, axis=-1, keepdims=True)
    return inverse * (upward - mean_up - normed * mean_cross)


def item_ids(ends, first_row, count):
    places = first_row + jnp.arange(count, dtype=jnp.int32)
    return jnp.sum((ends[:, None, :] <= places[None, :, None]).astype(jnp.int32), axis=2)


def block_size():
    return 512


def project(value_rows, weight_matrix):
    return jnp.einsum("srd,de->sre", value_rows, weight_matrix, preferred_element_type=jnp.float32)


def project_back(value_rows, weight_matrix):
    return jnp.einsum("sre,de->srd", value_rows, weight_matrix, preferred_element_type=jnp.float32)


def outer_sum(left, right):
    return jnp.einsum("srd,sre->de", left, right, preferred_element_type=jnp.float32)


def column_sum(value_rows):
    return jnp.sum(value_rows.astype(jnp.float32), axis=(0, 1))


def score_pieces(
    query_block,
    query_block_ids,
    logsum_block,
    correction_block,
    attended_block,
    keys_block,
    values_block,
    key_ids,
):
    matching = (query_block_ids[:, :, None] == key_ids[:, None, :])[:, :, None, :]
    scores = jnp.einsum(
        "sqhe,skhe->sqhk", query_block, keys_block, preferred_element_type=jnp.float32
    )
    weights = jnp.where(
        matching, jnp.exp(jnp.where(matching, scores, NEGATIVE) - logsum_block[..., None]), 0.0
    )
    upstream = jnp.einsum(
        "sqhe,skhe->sqhk", attended_block, values_block, preferred_element_type=jnp.float32
    )
    score_back = (weights * (upstream - correction_block[..., None])).astype(jnp.bfloat16)
    return (weights, score_back)


def absorb(state, pieces, queries, query_ids, ends):
    keys_piece, values_piece = pieces
    streams = keys_piece.shape[0]
    count = keys_piece.shape[1]
    width = block_size()

    def step(running, block_index):
        highest, total, accum = running
        keys_block = lax.dynamic_slice_in_dim(keys_piece, block_index * width, width, 1).reshape(
            streams, width, HEADS, HD
        )
        values_block = lax.dynamic_slice_in_dim(
            values_piece, block_index * width, width, 1
        ).reshape(streams, width, HEADS, HD)
        key_ids = item_ids(ends, block_index * width, width)
        matching = (query_ids[:, :, None] == key_ids[:, None, :])[:, :, None, :]
        scores = jnp.einsum(
            "sqhe,skhe->sqhk", queries, keys_block, preferred_element_type=jnp.float32
        )
        scores = jnp.where(matching, scores, NEGATIVE)
        new_high = jnp.maximum(highest, jnp.max(scores, axis=-1))
        weights = jnp.where(matching, jnp.exp(scores - new_high[..., None]), 0.0)
        factor = jnp.exp(highest - new_high)
        total = total * factor + jnp.sum(weights, axis=-1)
        accum = accum * factor[..., None] + jnp.einsum(
            "sqhk,skhe->sqhe",
            weights.astype(jnp.bfloat16),
            values_block,
            preferred_element_type=jnp.float32,
        )
        return ((new_high, total, accum), None)

    state, _ = lax.scan(step, state, jnp.arange(count // width, dtype=jnp.int32))
    return state


def body(
    tokens,
    query_weight,
    query_bias,
    key_weight,
    value_weight,
    value_bias,
    out_weight,
    out_bias,
    first_gain,
    attention_norm_shift,
    expand_weight,
    expand_bias,
    reduce_weight,
    reduce_bias,
    second_gain,
    second_shift,
    lengths,
    cotangent,
):
    masters = (
        query_weight,
        query_bias,
        key_weight,
        value_weight,
        value_bias,
        out_weight,
        out_bias,
        first_gain,
        attention_norm_shift,
        expand_weight,
        expand_bias,
        reduce_weight,
        reduce_bias,
        second_gain,
        second_shift,
    )
    casted = [entry.astype(jnp.bfloat16) for entry in masters]
    gathered = (
        lax.all_gather(casted[0], ("dp", "seq"), axis=0, tiled=True),
        lax.all_gather(casted[1], ("dp", "seq"), axis=0, tiled=True),
        lax.all_gather(casted[2], ("dp", "seq"), axis=0, tiled=True),
        lax.all_gather(casted[3], ("dp", "seq"), axis=0, tiled=True),
        lax.all_gather(casted[4], ("dp", "seq"), axis=0, tiled=True),
        lax.all_gather(casted[5], ("dp", "seq"), axis=0, tiled=True),
        lax.all_gather(casted[6], ("dp", "seq"), axis=0, tiled=True),
        lax.all_gather(casted[7], ("dp", "seq"), axis=0, tiled=True),
        lax.all_gather(casted[8], ("dp", "seq"), axis=0, tiled=True),
        lax.all_gather(casted[9], ("dp", "seq"), axis=0, tiled=True),
        lax.all_gather(casted[10], ("dp", "seq"), axis=0, tiled=True),
        lax.all_gather(casted[11], ("dp", "seq"), axis=0, tiled=True),
        lax.all_gather(casted[12], ("dp", "seq"), axis=0, tiled=True),
        lax.all_gather(casted[13], ("dp", "seq"), axis=0, tiled=True),
        lax.all_gather(casted[14], ("dp", "seq"), axis=0, tiled=True),
    )
    (
        query_weight,
        query_bias,
        key_weight,
        value_weight,
        value_bias,
        out_weight,
        out_bias,
        first_gain,
        attention_norm_shift,
        expand_weight,
        expand_bias,
        reduce_weight,
        reduce_bias,
        second_gain,
        second_shift,
    ) = gathered
    streams = tokens.shape[0]
    row_count = tokens.shape[1]
    ends = jnp.cumsum(lengths, axis=1)
    query_ids = item_ids(ends, lax.axis_index("seq") * row_count, row_count)
    queries = ((project(tokens, query_weight) + query_bias.astype(jnp.float32)) * 0.125).astype(
        jnp.bfloat16
    )
    key_low = project(tokens, key_weight).astype(jnp.bfloat16)
    value_low = (project(tokens, value_weight) + value_bias.astype(jnp.float32)).astype(
        jnp.bfloat16
    )
    queries_heads = queries.reshape(streams, row_count, HEADS, HD)
    initial = (
        jnp.full((streams, row_count, HEADS), NEGATIVE, jnp.float32),
        jnp.zeros((streams, row_count, HEADS), jnp.float32),
        jnp.zeros((streams, row_count, HEADS, HD), jnp.float32),
    )
    highest, total, accum = absorb(
        initial,
        (
            lax.all_gather(key_low, "seq", axis=1, tiled=True),
            lax.all_gather(value_low, "seq", axis=1, tiled=True),
        ),
        queries_heads,
        query_ids,
        ends,
    )
    logsum = highest + jnp.log(total)
    attended_full = accum / total[..., None]
    attended = attended_full.astype(jnp.bfloat16).reshape(streams, row_count, D)
    branch = project(attended, out_weight) + out_bias.astype(jnp.float32)
    normed_one, inverse_one = norm_rows(tokens.astype(jnp.float32) + branch)
    first = normed_one * first_gain.astype(jnp.float32) + attention_norm_shift.astype(jnp.float32)
    first_low = first.astype(jnp.bfloat16)
    expanded = project(first_low, expand_weight) + expand_bias.astype(jnp.float32)
    hidden = jax.nn.gelu(expanded, approximate=False).astype(jnp.bfloat16)
    reduced = project(hidden, reduce_weight) + reduce_bias.astype(jnp.float32)
    second_normed_rows, inverse_two = norm_rows(first + reduced)
    activations = (
        second_normed_rows * second_gain.astype(jnp.float32) + second_shift.astype(jnp.float32)
    ).astype(jnp.bfloat16)
    upward = cotangent.astype(jnp.float32)
    second_gain_grad = jnp.sum(upward * second_normed_rows, axis=(0, 1))
    second_shift_grad = jnp.sum(upward, axis=(0, 1))
    residual_two_back = norm_back(
        upward * second_gain.astype(jnp.float32), second_normed_rows, inverse_two
    )
    reduced_back = residual_two_back.astype(jnp.bfloat16)
    reduce_weight_grad = outer_sum(hidden, reduced_back)
    reduce_bias_grad = column_sum(reduced_back)
    hidden_back = project_back(reduced_back, reduce_weight)
    _, gelu_pull = jax.vjp(lambda inner: jax.nn.gelu(inner, approximate=False), expanded)
    expanded_back = gelu_pull(hidden_back)[0].astype(jnp.bfloat16)
    expand_weight_grad = outer_sum(first_low, expanded_back)
    expand_bias_grad = column_sum(expanded_back)
    first_back = project_back(expanded_back, expand_weight) + residual_two_back
    first_gain_grad = jnp.sum(first_back * normed_one, axis=(0, 1))
    first_shift_grad = jnp.sum(first_back, axis=(0, 1))
    residual_one_back = norm_back(
        first_back * first_gain.astype(jnp.float32), normed_one, inverse_one
    )
    branch_back = residual_one_back.astype(jnp.bfloat16)
    output_weight_gradient = outer_sum(attended, branch_back)
    out_bias_grad = column_sum(branch_back)
    attended_back = project_back(branch_back, out_weight).astype(jnp.bfloat16)
    attended_heads = attended_back.reshape(streams, row_count, HEADS, HD)
    correction = jnp.sum(attended_heads.astype(jnp.float32) * attended_full, axis=-1)
    again_keys, again_values = (
        lax.all_gather(key_low, "seq", axis=1, tiled=True),
        lax.all_gather(value_low, "seq", axis=1, tiled=True),
    )
    stream_rows = again_keys.shape[1]
    width = block_size()
    query_start = jnp.zeros((streams, row_count, HEADS, HD), jnp.float32)
    block_indices = jnp.arange(stream_rows // width, dtype=jnp.int32)

    def gradient_step(query_sum, block_index):
        keys_block = lax.dynamic_slice_in_dim(again_keys, block_index * width, width, 1).reshape(
            streams, width, HEADS, HD
        )
        values_block = lax.dynamic_slice_in_dim(
            again_values, block_index * width, width, 1
        ).reshape(streams, width, HEADS, HD)
        key_ids = item_ids(ends, block_index * width, width)
        weights, score_back = score_pieces(
            queries_heads,
            query_ids,
            logsum,
            correction,
            attended_heads,
            keys_block,
            values_block,
            key_ids,
        )
        query_sum = query_sum + jnp.einsum(
            "sqhk,skhe->sqhe", score_back, keys_block, preferred_element_type=jnp.float32
        )
        key_term = jnp.einsum(
            "sqhk,sqhe->skhe", score_back, queries_heads, preferred_element_type=jnp.float32
        )
        value_term = jnp.einsum(
            "sqhk,sqhe->skhe",
            weights.astype(jnp.bfloat16),
            attended_heads,
            preferred_element_type=jnp.float32,
        )
        return (
            query_sum,
            (key_term.reshape(streams, width, D), value_term.reshape(streams, width, D)),
        )

    query_sum, (key_terms, value_terms) = lax.scan(gradient_step, query_start, block_indices)
    key_terms = jnp.moveaxis(key_terms, 0, 1).reshape(streams, stream_rows, D)
    value_terms = jnp.moveaxis(value_terms, 0, 1).reshape(streams, stream_rows, D)
    key_total, value_total = (
        lax.psum_scatter(
            key_terms.astype(jnp.bfloat16), "seq", scatter_dimension=1, tiled=True
        ).astype(jnp.float32),
        lax.psum_scatter(
            value_terms.astype(jnp.bfloat16), "seq", scatter_dimension=1, tiled=True
        ).astype(jnp.float32),
    )
    key_back = key_total.astype(jnp.bfloat16)
    value_back = value_total.astype(jnp.bfloat16)
    query_back = query_sum.astype(jnp.bfloat16).reshape(streams, row_count, D) * jnp.bfloat16(0.125)
    gradients = (
        outer_sum(tokens, query_back),
        column_sum(query_back),
        outer_sum(tokens, key_back),
        outer_sum(tokens, value_back),
        column_sum(value_back),
        output_weight_gradient,
        out_bias_grad,
        first_gain_grad,
        first_shift_grad,
        expand_weight_grad,
        expand_bias_grad,
        reduce_weight_grad,
        reduce_bias_grad,
        second_gain_grad,
        second_shift_grad,
    )
    tokens_gradient = (
        residual_one_back
        + project_back(query_back, query_weight)
        + project_back(key_back, key_weight)
        + project_back(value_back, value_weight)
    )
    owned = (
        lax.psum_scatter(gradients[0], ("dp", "seq"), scatter_dimension=0, tiled=True),
        lax.psum_scatter(gradients[1], ("dp", "seq"), scatter_dimension=0, tiled=True),
        lax.psum_scatter(gradients[2], ("dp", "seq"), scatter_dimension=0, tiled=True),
        lax.psum_scatter(gradients[3], ("dp", "seq"), scatter_dimension=0, tiled=True),
        lax.psum_scatter(gradients[4], ("dp", "seq"), scatter_dimension=0, tiled=True),
        lax.psum_scatter(gradients[5], ("dp", "seq"), scatter_dimension=0, tiled=True),
        lax.psum_scatter(gradients[6], ("dp", "seq"), scatter_dimension=0, tiled=True),
        lax.psum_scatter(gradients[7], ("dp", "seq"), scatter_dimension=0, tiled=True),
        lax.psum_scatter(gradients[8], ("dp", "seq"), scatter_dimension=0, tiled=True),
        lax.psum_scatter(gradients[9], ("dp", "seq"), scatter_dimension=0, tiled=True),
        lax.psum_scatter(gradients[10], ("dp", "seq"), scatter_dimension=0, tiled=True),
        lax.psum_scatter(gradients[11], ("dp", "seq"), scatter_dimension=0, tiled=True),
        lax.psum_scatter(gradients[12], ("dp", "seq"), scatter_dimension=0, tiled=True),
        lax.psum_scatter(gradients[13], ("dp", "seq"), scatter_dimension=0, tiled=True),
        lax.psum_scatter(gradients[14], ("dp", "seq"), scatter_dimension=0, tiled=True),
    )
    return (
        activations,
        tokens_gradient,
        owned[0],
        owned[1],
        owned[2],
        owned[3],
        owned[4],
        owned[5],
        owned[6],
        owned[7],
        owned[8],
        owned[9],
        owned[10],
        owned[11],
        owned[12],
        owned[13],
        owned[14],
    )


def solution(mesh):
    placed = (
        P("dp", "seq", None),
        P(("dp", "seq"), None),
        P(("dp", "seq")),
        P(("dp", "seq"), None),
        P(("dp", "seq"), None),
        P(("dp", "seq")),
        P(("dp", "seq"), None),
        P(("dp", "seq")),
        P(("dp", "seq")),
        P(("dp", "seq")),
        P(("dp", "seq"), None),
        P(("dp", "seq")),
        P(("dp", "seq"), None),
        P(("dp", "seq")),
        P(("dp", "seq")),
        P(("dp", "seq")),
        P("dp", None),
        P("dp", "seq", None),
    )
    return jax.shard_map(
        body,
        mesh=mesh,
        in_specs=placed,
        out_specs=(
            P("dp", "seq", None),
            P("dp", "seq", None),
            P(("dp", "seq"), None),
            P(("dp", "seq")),
            P(("dp", "seq"), None),
            P(("dp", "seq"), None),
            P(("dp", "seq")),
            P(("dp", "seq"), None),
            P(("dp", "seq")),
            P(("dp", "seq")),
            P(("dp", "seq")),
            P(("dp", "seq"), None),
            P(("dp", "seq")),
            P(("dp", "seq"), None),
            P(("dp", "seq")),
            P(("dp", "seq")),
            P(("dp", "seq")),
        ),
        check_vma=False,
    )
```

profile of v0, /device:TPU:13, one launch (start us, length us, event | category | flops | bytes accessed | tf_op | source)
XLA Modules:
  0.0 1314.1 jit_solution(423696589849540586)
XLA Ops:
  19.9 40.0 %all-reduce.19 = (bf16[3072]{0:T(1024)(128)(2,1)S(1)}, bf16[768]{0:T(1024)(128)(2,1)S(1)}, bf16[768]{0:T(1024)(128)(2,1)S(1)}, bf16[768]{0:T(1024)(128)(2,1)S(1)...) all-reduce(bf16[3072]{0:T(1024)(128)(2,1)S(1)} %dynamic-update-slic, ...), channel_id=1, replica_groups=mesh['dp'=4,'seq'=8] {'dp','seq'}, use_global_device_ids=true, to_apply=%add.5 | all-reduce | flops 9216 | bytes 36864
  59.9 6.6 all-gather.15.cloned.1.call-done
  66.5 2.7 fusion.64
  69.3 54.4 %all-gather.9.cloned.1.call-done = bf16[768,768]{1,0:T(8,128)(2,1)} async-done(((bf16[24,768]{1,0:T(8,128)(2,1)}), bf16[768,768]{1,0:T(8,128)(2,1)}) %all-gather.9.cloned.1.call-update) | async-done | bytes 1179664 | tf_op jit(solution)/shard_map/all_gather | solution.py:154
  123.6 2.5 convolution_convert_fusion.1
  131.2 49.2 %all-gather.13.cloned.1.call-done = bf16[768,768]{1,0:T(8,128)(2,1)} async-done(((bf16[24,768]{1,0:T(8,128)(2,1)}), bf16[768,768]{1,0:T(8,128)(2,1)}) %all-gather.13.cloned.1.call-update) | async-done | bytes 1179664 | tf_op jit(solution)/shard_map/all_gather | solution.py:152
  180.4 1.7 fusion.63
  182.3 36.7 %all-gather.17.cloned.1.call-done = bf16[2,1024,768]{2,1,0:T(8,128)(2,1)} async-done(((bf16[2,128,768]{2,1,0:T(8,128)(2,1)}), bf16[2,1024,768]{2,1,0:T(8,128)(2,1)}) %all-gather.17.cloned.1.call-update) | async-done | bytes 3145744 | tf_op jit(solution)/shard_map/all_gather | solution.py:206
  219.0 4.6 copy.104
  223.7 34.6 %all-gather.11.cloned.1.call-done = bf16[2,1024,768]{2,1,0:T(8,128)(2,1)} async-done(((bf16[2,128,768]{2,1,0:T(8,128)(2,1)}), bf16[2,1024,768]{2,1,0:T(8,128)(2,1)}) %all-gather.11.cloned.1.call-update) | async-done | bytes 3145744 | tf_op jit(solution)/shard_map/all_gather | solution.py:205
  258.2 4.7 copy.103
  262.9 28.5 %while.30 = (s32[]{:T(128)}, f32[2,128,12]{1,2,0:T(8,128)S(1)}, f32[2,128,12]{1,2,0:T(8,128)S(1)}, f32[2,128,12,64]{1,3,2,0:T(8,128)S(1)}, s32[2,128]{1,0:T(2,12...) while((s32[]{:T(128)}, f32[2,128,12]{1,2,0:T(8,128)S(1)}, ...), condition=%wide.region_6.7_spmd.clone, body=%wide.region_2.6_spmd.clone.sunk | while | flops 419314176 | bytes 56178412 | solution.py:109
  264.2 2.1 constant_dynamic-slice_fusion.7
  266.6 3.9 fusion.156
  270.5 4.2 fusion.157
  275.1 2.0 fusion.159
  278.4 2.1 constant_dynamic-slice_fusion.7
  280.8 3.9 fusion.156
  284.8 4.2 fusion.157
  289.4 2.0 fusion.159
  291.5 23.3 %all-gather.19.cloned.1.call-done = bf16[768,768]{1,0:T(8,128)(2,1)} async-done(((bf16[24,768]{1,0:T(8,128)(2,1)}), bf16[768,768]{1,0:T(8,128)(2,1)}) %all-gather.19.cloned.1.call-update) | async-done | bytes 1179664 | tf_op jit(solution)/shard_map/all_gather | solution.py:157
  314.9 1.9 fusion.91
  317.6 64.8 %all-gather.21.cloned.1.call-done = bf16[768,3072]{1,0:T(8,128)(2,1)} async-done(((bf16[24,3072]{1,0:T(8,128)(2,1)}), bf16[768,3072]{1,0:T(8,128)(2,1)}) %all-gather.21.cloned.1.call-update) | async-done | bytes 4718608 | tf_op jit(solution)/shard_map/all_gather | solution.py:161
  382.4 4.8 fusion.81
  388.9 8.1 multiply_convert_fusion
  397.0 51.5 %all-gather.23.cloned.1.call-done = bf16[3072,768]{1,0:T(8,128)(2,1)} async-done(((bf16[96,768]{1,0:T(8,128)(2,1)}), bf16[3072,768]{1,0:T(8,128)(2,1)}) %all-gather.23.cloned.1.call-update) | async-done | bytes 4718608 | tf_op jit(solution)/shard_map/all_gather | solution.py:163
  448.6 4.0 fusion.92
  455.5 2.7 convert_reduce_fusion.2
  458.3 2.4 multiply_reduce_fusion
  463.1 1.7 multiply_reduce_fusion.1
  464.9 63.9 %while.31 = (s32[]{:T(128)}, f32[2,128,12,64]{1,3,2,0:T(8,128)}, bf16[2,2,512,768]{3,2,0,1:T(8,128)(2,1)}, bf16[2,2,512,768]{3,2,0,1:T(8,128)(2,1)}, s32[2]{0:T(...) while((s32[]{:T(128)}, f32[2,128,12,64]{1,3,2,0:T(8,128)}, ...), condition=%wide.region_18.19_spmd.clone, body=%wide.region_16.18_spmd.clone.sunk | while | flops 1023081984 | bytes 97067584 | solution.py:296
  469.0 2.8 constant_dynamic-slice_fusion.9
  472.1 3.6 fusion.171
  475.8 1.7 copy-done.1
  477.5 2.4 fusion.174
  481.6 5.8 fusion.173
  487.4 2.6 copy.159
  490.0 3.3 constant_dynamic-update-slice_fusion.3
  493.3 3.5 fusion.172
  500.7 2.8 constant_dynamic-slice_fusion.9
  503.9 3.6 fusion.171
  507.5 1.7 copy-done.1
  509.2 2.4 fusion.174
  513.3 5.8 fusion.173
  519.1 2.6 copy.159
  521.7 3.4 constant_dynamic-update-slice_fusion.3
  525.1 3.7 fusion.172
  531.9 2.0 copy.129
  534.0 1.9 convolution_bitcast_fusion.3
  536.0 29.2 %reduce-scatter.15.cloned.1.call-done = bf16[2,128,768]{2,1,0:T(8,128)(2,1)} async-done(((bf16[2,1024,768]{2,1,0:T(8,128)(2,1)}), bf16[2,128,768]{2,1,0:T(8,128)(2,1)}) %reduce-scatter.15.cloned.1.call-update) | async-done | bytes 393232 | tf_op jit(solution)/shard_map/reduce_scatter | solution.py:300
  566.7 2.0 copy.131
  568.7 38.0 %reduce-scatter.17.cloned.1.call-done = bf16[2,128,768]{2,1,0:T(8,128)(2,1)} async-done(((bf16[2,1024,768]{2,1,0:T(8,128)(2,1)}), bf16[2,128,768]{2,1,0:T(8,128)(2,1)}) %reduce-scatter.17.cloned.1.call-update) | async-done | bytes 393232 | tf_op jit(solution)/shard_map/reduce_scatter | solution.py:303
  608.3 2.0 copy.133
  611.7 5.2 convolution_bitcast_fusion.2
  618.5 5.1 convolution_bitcast_fusion.1
  625.1 2.8 convolution_add_fusion.2
  628.0 41.6 %all-reduce.18 = (f32[768]{0:T(1024)S(1)}, f32[768]{0:T(1024)S(1)}, f32[768]{0:T(1024)S(1)}, f32[768]{0:T(1024)S(1)}, f32[768]{0:T(1024)S(1)}, /*index=5*/f32[30...) all-reduce(f32[768]{0:T(1024)} %reduce_sum.211, ...), channel_id=5, replica_groups=mesh['dp'=4,'seq'=8] {'dp','seq'}, use_global_device_ids=true, to_apply=%region_23.24.clone | all-reduce | flops 9216 | bytes 73728
  674.9 1.8 convolution_add_fusion.1
  678.1 33.5 %reduce-scatter.25.cloned.1.call-done = f32[24,768]{1,0:T(8,128)} async-done(((f32[768,768]{1,0:T(8,128)}), f32[24,768]{1,0:T(8,128)}) %reduce-scatter.25.cloned.1.call-update) | async-done | bytes 73744
  711.5 104.7 %reduce-scatter.19.cloned.1.call-done = f32[24,768]{1,0:T(8,128)} async-done(((f32[768,768]{1,0:T(8,128)}), f32[24,768]{1,0:T(8,128)}) %reduce-scatter.19.cloned.1.call-update) | async-done | bytes 73744 | tf_op jit(solution)/shard_map/reduce_scatter | solution.py:339
  816.2 103.9 %reduce-scatter.27.cloned.1.call-done = f32[24,768]{1,0:T(8,128)} async-done(((f32[768,768]{1,0:T(8,128)}), f32[24,768]{1,0:T(8,128)}) %reduce-scatter.27.cloned.1.call-update) | async-done | bytes 73744
  920.1 104.6 %reduce-scatter.29.cloned.1.call-done = f32[24,768]{1,0:T(8,128)} async-done(((f32[768,768]{1,0:T(8,128)}), f32[24,768]{1,0:T(8,128)}) %reduce-scatter.29.cloned.1.call-update) | async-done | bytes 73744
  1024.7 140.6 %reduce-scatter.21.cloned.1.call-done = f32[24,3072]{1,0:T(8,128)} async-done(((f32[768,3072]{1,0:T(8,128)}), f32[24,3072]{1,0:T(8,128)}) %reduce-scatter.21.cloned.1.call-update) | async-done | bytes 294928 | tf_op jit(solution)/shard_map/reduce_scatter | solution.py:343
  1165.4 141.9 %reduce-scatter.23.cloned.1.call-done = f32[96,768]{1,0:T(8,128)} async-done(((f32[3072,768]{1,0:T(8,128)}), f32[96,768]{1,0:T(8,128)}) %reduce-scatter.23.cloned.1.call-update) | async-done | bytes 294928 | tf_op jit(solution)/shard_map/reduce_scatter | solution.py:345
  (297 shorter events, 56.0 us)
Async XLA Ops:
  7.2 116.4 %copy-start.6 = (bf16[2,128,768]{2,1,0:T(8,128)(2,1)S(1)}, bf16[2,128,768]{2,1,0:T(8,128)(2,1)}, u32[]{:S(2)}) copy-start(bf16[2,128,768]{2,1,0:T(8,128)(2,1)} %param.22) | copy-start | bytes 1179652
  7.2 119.0 %copy-start.44 = (f32[24,768]{1,0:T(8,128)S(1)}, f32[24,768]{1,0:T(8,128)}, u32[]{:S(2)}) copy-start(f32[24,768]{1,0:T(8,128)} %param.28) | copy-start | bytes 221188
  7.2 119.7 %copy-start.33 = (f32[24,3072]{1,0:T(8,128)S(1)}, f32[24,3072]{1,0:T(8,128)}, u32[]{:S(2)}) copy-start(f32[24,3072]{1,0:T(8,128)} %param.32) | copy-start | bytes 884740
  7.2 120.4 %copy-start.34 = (f32[96,768]{1,0:T(8,128)S(1)}, f32[96,768]{1,0:T(8,128)}, u32[]{:S(2)}) copy-start(f32[96,768]{1,0:T(8,128)} %param.34) | copy-start | bytes 884740
  7.2 59.3 %all-gather.15.cloned.1.call-start = ((), (), s32[]{:S(2)}) async-start(), calls=%async_computation.11 | async-start | bytes 1216512 | tf_op jit(solution)/shard_map/all_gather | solution.py:155
  8.9 114.7 %all-gather.9.cloned.1.call-start = ((), (), s32[]{:S(2)}) async-start(), calls=%async_computation.8 | async-start | bytes 1216512 | tf_op jit(solution)/shard_map/all_gather | solution.py:154
  10.5 169.9 %all-gather.13.cloned.1.call-start = ((), (), s32[]{:S(2)}) async-start(), calls=%async_computation.10 | async-start | bytes 1216512 | tf_op jit(solution)/shard_map/all_gather | solution.py:152
  12.0 207.0 %all-gather.17.cloned.1.call-start = ((), (), s32[]{:S(2)}) async-start(), calls=%async_computation.12 | async-start | bytes 3538944 | tf_op jit(solution)/shard_map/all_gather | solution.py:206
  59.9 69.1 %copy-start.59 = (s32[2,64]{1,0:T(2,128)S(1)}, s32[2,64]{1,0:T(2,128)}, u32[]{:S(2)}) copy-start(s32[2,64]{1,0:T(2,128)} %param.38) | copy-start | bytes 1540
  69.2 189.0 %all-gather.11.cloned.1.call-start = ((), (), s32[]{:S(2)}) async-start(), calls=%async_computation.9 | async-start | bytes 3538944 | tf_op jit(solution)/shard_map/all_gather | solution.py:205
  126.1 188.7 %all-gather.19.cloned.1.call-start = ((), (), s32[]{:S(2)}) async-start(), calls=%async_computation.13 | async-start | bytes 1216512 | tf_op jit(solution)/shard_map/all_gather | solution.py:157
  126.8 255.6 %all-gather.21.cloned.1.call-start = ((), (), s32[]{:S(2)}) async-start(), calls=%async_computation.14 | async-start | bytes 4866048 | tf_op jit(solution)/shard_map/all_gather | solution.py:161
  127.6 320.9 %all-gather.23.cloned.1.call-start = ((), (), s32[]{:S(2)}) async-start(), calls=%async_computation.15 | async-start | bytes 4866048 | tf_op jit(solution)/shard_map/all_gather | solution.py:163
  128.4 436.8 %reduce-scatter.15.cloned.1.call-start = ((), (), s32[]{:S(2)}) async-start(), calls=%async_computation.16 | async-start | bytes 3538944 | tf_op jit(solution)/shard_map/reduce_scatter | solution.py:300
  129.3 253.2 %copy-start.35 = (f32[768]{0:T(1024)}, f32[768]{0:T(1024)S(1)}, u32[]{:S(2)}) copy-start(f32[768]{0:T(1024)S(1)} %convert_element_type.192) | copy-start | bytes 9220
  129.3 253.2 %copy-start.42 = (f32[768]{0:T(1024)}, f32[768]{0:T(1024)S(1)}, u32[]{:S(2)}) copy-start(f32[768]{0:T(1024)S(1)} %convert_element_type.194) | copy-start | bytes 9220
  270.5 4.6 copy-start
  284.8 4.6 copy-start
  291.4 95.8 %copy-start.23 = (f32[2,128,12,64]{1,3,2,0:T(8,128)}, f32[2,128,12,64]{1,3,2,0:T(8,128)S(1)}, u32[]{:S(2)}) copy-start(f32[2,128,12,64]{1,3,2,0:T(8,128)S(1)} %get-tuple-element.140) | copy-start | bytes 2359300
  291.4 95.8 %copy-start.38 = (s32[2,64]{1,0:T(2,128)}, s32[2,64]{1,0:T(2,128)S(1)}, u32[]{:S(2)}) copy-start(s32[2,64]{1,0:T(2,128)S(1)} %get-tuple-element.780) | copy-start | bytes 1540
  291.4 95.8 %copy-start.40 = (s32[2,128]{1,0:T(2,128)}, s32[2,128]{1,0:T(2,128)S(1)}, u32[]{:S(2)}) copy-start(s32[2,128]{1,0:T(2,128)S(1)} %get-tuple-element.789) | copy-start | bytes 3076
  291.5 95.7 %copy-start.13 = (bf16[2,128,12,64]{1,3,2,0:T(8,128)(2,1)}, bf16[2,128,12,64]{1,3,2,0:T(8,128)(2,1)S(1)}, u32[]{:S(2)}) copy-start(bf16[2,128,12,64]{1,3,2,0:T(8,128)(2,1)S(1)} %fusion.83) | copy-start | bytes 1179652
  316.7 144.0 %copy-start.4 = (f32[2,128,768]{2,1,0:T(8,128)}, f32[2,128,768]{2,1,0:T(8,128)S(1)}, u32[]{:S(2)}) copy-start(f32[2,128,768]{2,1,0:T(8,128)S(1)} %get-tuple-element.473) | copy-start | bytes 2359300
  316.7 70.5 %copy-start.46 = (f32[2,128]{1,0:T(2,128)}, f32[2,128]{1,0:T(2,128)S(1)}, u32[]{:S(2)}) copy-start(f32[2,128]{1,0:T(2,128)S(1)} %broadcast_multiply_fusion.5) | copy-start | bytes 3076
  317.0 70.3 %copy-start.49 = (f32[2,128]{1,0:T(2,128)}, f32[2,128]{1,0:T(2,128)S(1)}, u32[]{:S(2)}) copy-start(f32[2,128]{1,0:T(2,128)S(1)} %add_rsqrt_fusion.1) | copy-start | bytes 3076
  397.0 55.5 %copy-start.8 = (bf16[2,128,3072]{2,1,0:T(8,128)(2,1)}, bf16[2,128,3072]{2,1,0:T(8,128)(2,1)S(1)}, u32[]{:S(2)}) copy-start(bf16[2,128,3072]{2,1,0:T(8,128)(2,1)S(1)} %get-tuple-element.463) | copy-start | bytes 4718596
  448.5 4.3 copy-start.29
  448.6 4.3 copy-start.45
  448.6 5.2 copy-start.53
  448.6 6.9 copy-start.22
  448.6 6.9 copy-start.60
  452.6 2.9 copy-start.21
  453.8 4.5 slice-start
  458.3 3.3 copy-start.11
  461.6 3.2 copy-start.15
  465.1 3.8 copy-start.61
  468.9 6.8 copy-start.2
  468.9 2.9 copy-start.39
  468.9 3.0 copy-start.41
  468.9 3.2 copy-start.52
  468.9 3.2 copy-start.55
  472.1 3.6 copy-start.19
  477.5 4.1 copy-start.56
  493.3 3.5 copy-start.62
  496.8 3.8 copy-start.61
  500.6 6.8 copy-start.2
  500.6 2.9 copy-start.39
  500.7 3.0 copy-start.41
  500.7 3.2 copy-start.52
  500.7 3.2 copy-start.55
  503.8 3.6 copy-start.19
  509.2 4.1 copy-start.56
  525.1 3.7 copy-start.62
  528.8 77.9 %reduce-scatter.17.cloned.1.call-start = ((), (), s32[]{:S(2)}) async-start(), calls=%async_computation.17 | async-start | bytes 3538944 | tf_op jit(solution)/shard_map/reduce_scatter | solution.py:303
  529.4 182.2 %reduce-scatter.25.cloned.1.call-start = ((), (), s32[]{:S(2)}) async-start(), calls=%async_computation.21 | async-start | bytes 2433024
  533.9 282.3 %reduce-scatter.19.cloned.1.call-start = ((), (), s32[]{:S(2)}) async-start(), calls=%async_computation.18 | async-start | bytes 2433024 | tf_op jit(solution)/shard_map/reduce_scatter | solution.py:339
  536.0 384.1 %reduce-scatter.27.cloned.1.call-start = ((), (), s32[]{:S(2)}) async-start(), calls=%async_computation.22 | async-start | bytes 2433024
  568.7 456.0 %reduce-scatter.29.cloned.1.call-start = ((), (), s32[]{:S(2)}) async-start(), calls=%async_computation.23 | async-start | bytes 2433024
  610.4 555.0 %reduce-scatter.21.cloned.1.call-start = ((), (), s32[]{:S(2)}) async-start(), calls=%async_computation.19 | async-start | bytes 9732096 | tf_op jit(solution)/shard_map/reduce_scatter | solution.py:343
  617.0 690.3 %reduce-scatter.23.cloned.1.call-start = ((), (), s32[]{:S(2)}) async-start(), calls=%async_computation.20 | async-start | bytes 9732096 | tf_op jit(solution)/shard_map/reduce_scatter | solution.py:345
  623.6 4.4 copy-start.12
  623.6 4.4 copy-start.54
  623.6 51.3 %copy-start.10 = (bf16[768,768]{1,0:T(8,128)(2,1)S(1)}, bf16[768,768]{1,0:T(8,128)(2,1)}, u32[]{:S(2)}) copy-start(bf16[768,768]{1,0:T(8,128)(2,1)} %all-gather.9.cloned.1.call-done) | copy-start | bytes 3538948
  627.9 48.8 %copy-start.32 = (bf16[768,768]{1,0:T(8,128)(2,1)S(1)}, bf16[768,768]{1,0:T(8,128)(2,1)}, u32[]{:S(2)}) copy-start(bf16[768,768]{1,0:T(8,128)(2,1)} %all-gather.15.cloned.1.call-done) | copy-start | bytes 3538948
  (28 other events, 54.9 us)
Sparse Core Ops, SparseCore 0:
  11.7 54.8 all-gather.14
  70.1 53.4 all-gather.8
  127.2 53.1 all-gather.12
  181.8 37.1 all-gather.16
  221.1 37.1 all-gather.10
  261.7 53.1 all-gather.18
  318.5 63.9 all-gather.20
  386.0 62.4 all-gather.22
  528.9 36.2 reduce-scatter.14
  567.3 39.3 reduce-scatter.16
  612.6 98.8 reduce-scatter.24
  718.1 98.0 reduce-scatter.18
  822.1 97.9 reduce-scatter.26
  926.7 98.0 reduce-scatter.28
  1031.0 134.2 reduce-scatter.20
  1172.7 134.5 reduce-scatter.22
where the time goes:
time: 1320 us; the launch traced here: 1310 us
  waiting for transfers between devices  1020 us (77%)
  matrix products  89.5 us (7%)
  blocking collectives  81.7 us (6%)
  local copies, waits for them, and re-layouts  65.2 us (5%)
  other arithmetic  39.8 us (3%)
  between operations  15 us (1%)
    unnamed x19, waiting for transfers between devices  243 us
    reduce_scatter x1, waiting for transfers between devices, body(): lax.psum_scatter(gradients[11], ('dp', 'seq'), scatter_dimension=0, tiled...  142 us
    reduce_scatter x1, waiting for transfers between devices, body(): lax.psum_scatter(gradients[9], ('dp', 'seq'), scatter_dimension=0, tiled=...  141 us
    reduce_scatter x1, waiting for transfers between devices, body(): lax.psum_scatter(gradients[5], ('dp', 'seq'), scatter_dimension=0, tiled=...  105 us
    unnamed x2, blocking collectives  81.7 us
    all_gather x1, waiting for transfers between devices, body(): lax.all_gather(casted[9], ('dp', 'seq'), axis=0, tiled=True)  64.8 us
    all_gather x1, waiting for transfers between devices, body(): lax.all_gather(casted[2], ('dp', 'seq'), axis=0, tiled=True)  54.4 us
    all_gather x1, waiting for transfers between devices, body(): lax.all_gather(casted[11], ('dp', 'seq'), axis=0, tiled=True)  51.5 us
  transfers between devices with their start and end apart: 16, of which 16 were waited for; matrix products, arithmetic and copies ran while one was open for 8% of the time, Pallas kernels for 0%

commit v1 on v0

v1 whole, which is shorter than its diff:
```python
import functools

import jax
import jax.numpy as jnp
from jax import lax
from jax.experimental import pallas as pl
from jax.experimental.pallas import tpu as pltpu
from jax.sharding import PartitionSpec as P

D = 768
HEADS = 12
HD = 64
FF = 3072
PAIR = 2 * HD
PAIRS = HEADS // 2
NEGATIVE = -1e30
EPSILON = 1e-12
BF = jnp.bfloat16
F32 = jnp.float32
VMEM_LIMIT = 56 * 1024 * 1024


def nn(left, right):
    return lax.dot_general(left, right, (((1,), (0,)), ((), ())), preferred_element_type=F32)


def nt(left, right):
    return lax.dot_general(left, right, (((1,), (1,)), ((), ())), preferred_element_type=F32)


def tn(left, right):
    return lax.dot_general(left, right, (((0,), (0,)), ((), ())), preferred_element_type=F32)


def stacked_heads(pair_rows):
    lanes = lax.broadcasted_iota(jnp.int32, pair_rows.shape, 1)
    zero = jnp.zeros_like(pair_rows)
    return jnp.concatenate(
        [jnp.where(lanes < HD, pair_rows, zero), jnp.where(lanes < HD, zero, pair_rows)], axis=0
    )


def unstacked_heads(stacked):
    rows = stacked.shape[0] // 2
    lanes = lax.broadcasted_iota(jnp.int32, (rows, PAIR), 1)
    return jnp.where(lanes < HD, stacked[:rows], stacked[rows:])


def forward_kernel(qid_ref, kid_ref, q_ref, k_ref, v_ref, out_ref, lse_ref):
    queries = stacked_heads(q_ref[0])
    rows = q_ref.shape[1]
    bias = jnp.where(qid_ref[0][:, :1] == kid_ref[0][:1, :], 0.0, NEGATIVE)
    scores = nt(queries, k_ref[0])
    scores = jnp.concatenate([scores[:rows] + bias, scores[rows:] + bias], axis=0)
    highest = jnp.max(scores, axis=-1, keepdims=True)
    weights = jnp.exp(scores - highest)
    total = jnp.sum(weights, axis=-1, keepdims=True)
    probs = (weights * (1.0 / total)).astype(BF)
    out_ref[0] = unstacked_heads(nn(probs, v_ref[0])).astype(BF)
    lse_ref[0, 0] = jnp.broadcast_to(highest + jnp.log(total), lse_ref.shape[2:])


def backward_kernel(
    qid_ref, kid_ref, q_ref, k_ref, v_ref, lse_ref, up_ref, dq_ref, dk_ref, dv_ref
):
    queries = stacked_heads(q_ref[0])
    upward = stacked_heads(up_ref[0])
    rows = q_ref.shape[1]
    bias = jnp.where(qid_ref[0][:, :1] == kid_ref[0][:1, :], 0.0, NEGATIVE)
    lse = lse_ref[0, 0][:, :1]
    scores = nt(queries, k_ref[0])
    scores = jnp.concatenate([scores[:rows] + bias, scores[rows:] + bias], axis=0)
    probs = jnp.exp(scores - lse)
    dprobs = nt(upward, v_ref[0])
    correction = jnp.sum(probs * dprobs, axis=-1, keepdims=True)
    dscores = (probs * (dprobs - correction)).astype(BF)
    dq_ref[0] = (unstacked_heads(nn(dscores, k_ref[0])).astype(BF).astype(F32) * 0.125).astype(BF)
    dk_ref[0] = tn(dscores, queries).astype(BF)
    dv_ref[0] = tn(probs.astype(BF), upward).astype(BF)


def attention_specs(rows, keys):
    return dict(
        qid=pl.BlockSpec((1, rows, 128), lambda s, p: (s, 0, 0)),
        kid=pl.BlockSpec((1, 8, keys), lambda s, p: (s, 0, 0)),
        row=pl.BlockSpec((1, rows, PAIR), lambda s, p: (s, 0, p)),
        key=pl.BlockSpec((1, keys, PAIR), lambda s, p: (s, 0, p)),
        lse=pl.BlockSpec((1, 1, 2 * rows, 128), lambda s, p: (s, p, 0, 0)),
    )


def attend(query_ids, key_ids, queries, keys, values):
    streams, rows, _ = queries.shape
    count = keys.shape[1]
    specs = attention_specs(rows, count)
    macs = streams * HEADS * rows * count * HD
    return pl.pallas_call(
        forward_kernel,
        grid=(streams, PAIRS),
        in_specs=[specs["qid"], specs["kid"], specs["row"], specs["key"], specs["key"]],
        out_specs=[specs["row"], specs["lse"]],
        out_shape=[
            jax.ShapeDtypeStruct((streams, rows, D), BF),
            jax.ShapeDtypeStruct((streams, PAIRS, 2 * rows, 128), F32),
        ],
        compiler_params=pltpu.CompilerParams(vmem_limit_bytes=VMEM_LIMIT),
        cost_estimate=pl.CostEstimate(
            flops=8 * macs, bytes_accessed=4 * streams * count * D, transcendentals=macs // HD
        ),
        name="attend",
    )(query_ids, key_ids, queries, keys, values)


def attend_back(query_ids, key_ids, queries, keys, values, lse, upward):
    streams, rows, _ = queries.shape
    count = keys.shape[1]
    specs = attention_specs(rows, count)
    macs = streams * HEADS * rows * count * HD
    return pl.pallas_call(
        backward_kernel,
        grid=(streams, PAIRS),
        in_specs=[
            specs["qid"],
            specs["kid"],
            specs["row"],
            specs["key"],
            specs["key"],
            specs["lse"],
            specs["row"],
        ],
        out_specs=[specs["row"], specs["key"], specs["key"]],
        out_shape=[
            jax.ShapeDtypeStruct((streams, rows, D), BF),
            jax.ShapeDtypeStruct((streams, count, D), BF),
            jax.ShapeDtypeStruct((streams, count, D), BF),
        ],
        compiler_params=pltpu.CompilerParams(vmem_limit_bytes=VMEM_LIMIT),
        cost_estimate=pl.CostEstimate(
            flops=20 * macs, bytes_accessed=8 * streams * count * D, transcendentals=macs // HD
        ),
        name="attend_back",
    )(query_ids, key_ids, queries, keys, values, lse, upward)


def norm_rows(value_rows):
    centre = jnp.mean(value_rows, axis=-1, keepdims=True)
    centred = value_rows - centre
    inverse = lax.rsqrt(jnp.mean(centred * centred, axis=-1, keepdims=True) + EPSILON)
    return (centred * inverse, inverse)


def norm_back(upward, normed, inverse):
    mean_up = jnp.mean(upward, axis=-1, keepdims=True)
    mean_cross = jnp.mean(upward * normed, axis=-1, keepdims=True)
    return inverse * (upward - mean_up - normed * mean_cross)


def column_sum(value_rows):
    return jnp.sum(value_rows.astype(F32), axis=0)


def item_ids(lengths, first_row, count):
    items = lengths.shape[1]
    slot = jnp.arange(items, dtype=jnp.int32)
    ends = jnp.sum(jnp.where(slot[:, None] <= slot[None, :], lengths[:, :, None], 0), axis=1)
    places = first_row + jnp.arange(count, dtype=jnp.int32)
    return jnp.sum((ends[:, None, :] <= places[None, :, None]).astype(jnp.int32), axis=2)


def body(
    tokens,
    query_weight,
    query_bias,
    key_weight,
    value_weight,
    value_bias,
    out_weight,
    out_bias,
    first_gain,
    attention_norm_shift,
    expand_weight,
    expand_bias,
    reduce_weight,
    reduce_bias,
    second_gain,
    second_shift,
    lengths,
    cotangent,
    *,
    devices,
):
    axes = ("dp", "seq")
    streams, row_count, _ = tokens.shape
    block = D // devices
    wide = FF // devices

    smalls = (
        query_bias,
        value_bias,
        out_bias,
        first_gain,
        attention_norm_shift,
        reduce_bias,
        second_gain,
        second_shift,
        expand_bias,
    )
    small = jnp.concatenate(smalls)
    small_size = small.shape[0]
    small = jnp.pad(small, (0, 8 * D - small_size)).reshape(8, D)
    early = jnp.concatenate([query_weight, key_weight, value_weight, small], axis=0).astype(BF)
    late = jnp.concatenate(
        [out_weight, reduce_weight] + [expand_weight[:, c * D : (c + 1) * D] for c in range(4)], axis=0
    ).astype(BF)

    all_tokens = lax.all_gather(tokens, "seq", axis=1, tiled=True)
    early = lax.all_gather(early, axes, axis=0)
    late = lax.all_gather(late, axes, axis=0)

    def rows_of(gathered, start, count):
        return gathered[:, start : start + count].reshape(devices * count, D)

    query_weight = rows_of(early, 0, block)
    key_weight = rows_of(early, block, block)
    value_weight = rows_of(early, 2 * block, block)
    small = early[:, 3 * block :].reshape(devices, 8 * D)[:, :small_size].astype(F32)

    def vector(index):
        return small[:, index * block : (index + 1) * block].reshape(1, D)

    query_bias, value_bias, out_bias, first_gain, attention_norm_shift, reduce_bias, second_gain, second_shift = (
        vector(i) for i in range(8)
    )
    expand_bias = small[:, 8 * block :].reshape(1, FF)
    out_weight = rows_of(late, 0, block)
    reduce_weight = rows_of(late, block, wide)
    expand_weight = (
        late[:, block + wide :].reshape(devices, 4, block, D).transpose(0, 2, 1, 3).reshape(D, FF)
    )

    stream_rows = all_tokens.shape[1]
    rows = streams * row_count
    flat_tokens = tokens.reshape(rows, D)
    flat_all = all_tokens.reshape(streams * stream_rows, D)
    key_ids = item_ids(lengths, 0, stream_rows)
    query_ids = item_ids(lengths, lax.axis_index("seq") * row_count, row_count)
    key_ids = jnp.broadcast_to(key_ids[:, None, :], (streams, 8, stream_rows))
    query_ids = jnp.broadcast_to(query_ids[:, :, None], (streams, row_count, 128))

    queries = ((nn(flat_tokens, query_weight) + query_bias) * 0.125).astype(BF)
    queries = queries.reshape(streams, row_count, D)
    keys = nn(flat_all, key_weight).astype(BF).reshape(streams, stream_rows, D)
    values = (nn(flat_all, value_weight) + value_bias).astype(BF).reshape(streams, stream_rows, D)
    attended, lse = attend(query_ids, key_ids, queries, keys, values)
    attended = attended.reshape(rows, D)

    branch = nn(attended, out_weight) + out_bias
    normed_one, inverse_one = norm_rows(flat_tokens.astype(F32) + branch)
    first = normed_one * first_gain + attention_norm_shift
    first_low = first.astype(BF)
    expanded = nn(first_low, expand_weight) + expand_bias
    hidden, gelu_pull = jax.vjp(lambda inner: jax.nn.gelu(inner, approximate=False), expanded)
    hidden = hidden.astype(BF)
    reduced = nn(hidden, reduce_weight) + reduce_bias
    normed_two, inverse_two = norm_rows(first + reduced)
    activations = (normed_two * second_gain + second_shift).astype(BF)

    upward = cotangent.reshape(rows, D).astype(F32)
    second_gain_grad = jnp.sum(upward * normed_two, axis=0)
    second_shift_grad = jnp.sum(upward, axis=0)
    residual_two_back = norm_back(upward * second_gain, normed_two, inverse_two)
    reduced_back = residual_two_back.astype(BF)
    reduce_weight_grad = tn(hidden, reduced_back).astype(BF)
    reduce_bias_grad = column_sum(reduced_back)
    expanded_back = gelu_pull(nt(reduced_back, reduce_weight))[0].astype(BF)
    expand_weight_grad = tn(first_low, expanded_back).astype(BF)
    expand_bias_grad = column_sum(expanded_back)
    wide_grads = jnp.concatenate(
        [reduce_weight_grad.reshape(devices, wide, D)]
        + [expand_weight_grad[:, c * D : (c + 1) * D].reshape(devices, block, D) for c in range(4)],
        axis=1,
    )
    wide_grads = lax.psum_scatter(wide_grads, axes, scatter_dimension=0).astype(F32)

    first_back = nt(expanded_back, expand_weight) + residual_two_back
    first_gain_grad = jnp.sum(first_back * normed_one, axis=0)
    first_shift_grad = jnp.sum(first_back, axis=0)
    residual_one_back = norm_back(first_back * first_gain, normed_one, inverse_one)
    branch_back = residual_one_back.astype(BF)
    out_weight_grad = tn(attended, branch_back).astype(BF)
    out_bias_grad = column_sum(branch_back)
    attended_back = nt(branch_back, out_weight).astype(BF).reshape(streams, row_count, D)

    query_back, key_back, value_back = attend_back(
        query_ids, key_ids, queries, keys, values, lse, attended_back
    )
    query_back = query_back.reshape(rows, D)
    key_back = key_back.reshape(streams * stream_rows, D)
    value_back = value_back.reshape(streams * stream_rows, D)
    tokens_part = (nt(key_back, key_weight) + nt(value_back, value_weight)).astype(BF)
    tokens_part = lax.psum_scatter(
        tokens_part.reshape(streams, stream_rows, D), "seq", scatter_dimension=1, tiled=True
    )
    tokens_gradient = (
        residual_one_back + nt(query_back, query_weight) + tokens_part.reshape(rows, D).astype(F32)
    ).reshape(streams, row_count, D)
    query_weight_grad = tn(flat_tokens, query_back).astype(BF)
    key_weight_grad = tn(flat_all, key_back).astype(BF)
    value_weight_grad = tn(flat_all, value_back).astype(BF)
    small_grads = [
        column_sum(query_back),
        column_sum(value_back),
        out_bias_grad,
        first_gain_grad,
        first_shift_grad,
        reduce_bias_grad,
        second_gain_grad,
        second_shift_grad,
        expand_bias_grad,
    ]
    small_grads = jnp.concatenate([g.reshape(devices, -1) for g in small_grads], axis=1).astype(BF)
    small_grads = jnp.pad(small_grads, ((0, 0), (0, 8 * D - small_size))).reshape(devices, 8, D)
    narrow_grads = jnp.concatenate(
        [
            g.reshape(devices, block, D)
            for g in (query_weight_grad, key_weight_grad, value_weight_grad, out_weight_grad)
        ]
        + [small_grads],
        axis=1,
    )
    narrow_grads = lax.psum_scatter(narrow_grads, axes, scatter_dimension=0).astype(F32)
    small = narrow_grads[4 * block :].reshape(8 * D)

    def piece(index):
        return small[index * block : (index + 1) * block]

    return (
        activations.reshape(streams, row_count, D),
        tokens_gradient,
        narrow_grads[:block],
        piece(0),
        narrow_grads[block : 2 * block],
        narrow_grads[2 * block : 3 * block],
        piece(1),
        narrow_grads[3 * block : 4 * block],
        piece(2),
        piece(3),
        piece(4),
        wide_grads[wide:].reshape(4, block, D).transpose(1, 0, 2).reshape(block, FF),
        small[8 * block : 8 * block + wide],
        wide_grads[:wide],
        piece(5),
        piece(6),
        piece(7),
    )


def solution(mesh):
    sharded = ("dp", "seq")
    matrix = P(sharded, None)
    vector = P(sharded)
    token = P("dp", "seq", None)
    params = (
        matrix,
        vector,
        matrix,
        matrix,
        vector,
        matrix,
        vector,
        vector,
        vector,
        matrix,
        vector,
        matrix,
        vector,
        vector,
        vector,
    )
    return jax.shard_map(
        functools.partial(body, devices=mesh.shape["dp"] * mesh.shape["seq"]),
        mesh=mesh,
        in_specs=(token,) + params + (P("dp", None), token),
        out_specs=(token, token) + params,
        check_vma=False,
    )
```

time: 1320 us -> 574 us (0.43)
  waiting for transfers between devices: 1020 us -> 376 us
  blocking collectives: 81.7 us -> 0 us
  matrix products: 89.5 us -> 52.5 us
  Pallas kernels: 0 us -> 29.7 us
  other arithmetic: 39.8 us -> 22.7 us
    unnamed x19 -> x6, waiting for transfers between devices: 243 us -> 0.1 us
    reduce_scatter x5 -> x3, waiting for transfers between devices: 454 us -> 241 us  [the longest x1 138 us: body(): lax.psum_scatter(wide_grads, axes, scatter_dimension=0).astype(F32)]
    all_gather x8 -> x3, waiting for transfers between devices: 321 us -> 135 us  [the longest x1 60.5 us: body(): early = lax.all_gather(early, axes, axis=0)]
    unnamed x2 -> x0, blocking collectives: 81.7 us -> none
    dot_general x32 -> x18, matrix products: 89.5 us -> 52.5 us  [the longest x6 22 us: nn(): lax.dot_general(left, right, (((1,), (0,)), ((), ())), preferred_element_...]
    pallas_call x0 -> x2, Pallas kernels: none -> 29.7 us  [the longest x1 16.6 us: attend_back(): pl.pallas_call(backward_kernel, grid=(streams, PAIRS), in_specs=[specs['q...]
    convert_element_type x26 -> x3, other arithmetic: 22.5 us -> 1.94 us  [the longest x1 1 us: body(): lax.psum_scatter(wide_grads, axes, scatter_dimension=0).astype(F32)]
    slice x0 -> x13, local copies, waits for them, and re-layouts: none -> 16.1 us  [the longest x3 10.3 us: rows_of(): return gathered[:, start:start + count].reshape(devices * count, D)]
  transfers between devices with their start and end apart: 16 -> 6, of which waited for: 16 -> 5; matrix products, arithmetic and copies ran while one was open for 8% -> 17% of each run, Pallas kernels for 0% -> 2%
where the time goes in v1:
time: 574 us; the launch traced here: 564 us
  waiting for transfers between devices  376 us (66%)
  local copies, waits for them, and re-layouts  67.7 us (12%)
  matrix products  52.5 us (9%)
  Pallas kernels  29.7 us (5%)
  other arithmetic  22.7 us (4%)
  between operations  15.1 us (3%)
    reduce_scatter x1, waiting for transfers between devices, body(): lax.psum_scatter(wide_grads, axes, scatter_dimension=0).astype(F32)  138 us
    reduce_scatter x1, waiting for transfers between devices, body(): lax.psum_scatter(narrow_grads, axes, scatter_dimension=0).astype(F32)  103 us
    all_gather x1, waiting for transfers between devices, body(): early = lax.all_gather(early, axes, axis=0)  60.5 us
    all_gather x1, waiting for transfers between devices, body(): late = lax.all_gather(late, axes, axis=0)  47.6 us
    all_gather x1, waiting for transfers between devices, body(): all_tokens = lax.all_gather(tokens, 'seq', axis=1, tiled=True)  26.8 us
    dot_general x6, matrix products, nn(): lax.dot_general(left, right, (((1,), (0,)), ((), ())), preferred_element_...  22 us
    dot_general x6, matrix products, nt(): lax.dot_general(left, right, (((1,), (1,)), ((), ())), preferred_element_...  17.5 us
    pallas_call x1, Pallas kernels, attend_back(): pl.pallas_call(backward_kernel, grid=(streams, PAIRS), in_specs=[specs['q...  16.6 us
  transfers between devices with their start and end apart: 6, of which 5 were waited for; matrix products, arithmetic and copies ran while one was open for 17% of the time, Pallas kernels for 2%

profile of v1, /device:TPU:13, one launch (start us, length us, event | category | flops | bytes accessed | tf_op | source)
XLA Modules:
  0.0 563.9 jit_solution(6658388620105908206)
XLA Ops:
  7.2 1.9 copy.54
  15.3 0.9 convert_bitcast_fusion.2
  16.2 0.9 convert_bitcast_fusion
  17.9 1.0 convert.117
  18.9 0.9 bitcast_dynamic-update-slice_fusion.1
  19.8 1.1 bitcast_dynamic-update-slice_fusion
  22.1 26.8 %all-gather.6.cloned.1.call-done = bf16[2,1024,768]{1,2,0:T(8,128)(2,1)} async-done(((bf16[2,128,768]{1,2,0:T(8,128)(2,1)}), bf16[2,1024,768]{1,2,0:T(8,128)(2,1)}) %all-gather.6.cloned.1.call-update) | async-done | bytes 3145744 | tf_op jit(solution)/shard_map/all_gather | solution.py:216
  48.8 4.7 copy.55
  53.5 60.5 %all-gather.4.cloned.1.call-done = bf16[32,80,768]{2,1,0:T(8,128)(2,1)} async-done(((bf16[1,80,768]{2,1,0:T(8,128)(2,1)}), bf16[32,80,768]{2,1,0:T(8,128)(2,1)}) %all-gather.4.cloned.1.call-update) | async-done | bytes 3932176 | tf_op jit(solution)/shard_map/all_gather | solution.py:217
  114.0 1.0 slice.191
  116.2 2.4 fusion.38
  118.6 1.0 copy-done.15
  119.6 4.1 fusion.6
  123.7 4.7 copy.56
  128.5 6.3 %fusion.7 = bf16[2048,768]{0,1:T(8,128)(2,1)} fusion(f32[768]{0:T(1024)S(1)} %add.131, bf16[768,768]{1,0:T(8,128)(2,1)S(1)} %bitcast.180, bf16[2048,768]{1,0:T(8,128)(2,1)} %bitcast.173), kind=kOutput, calls=%fused_computation.24 | convolution fusion | flops 2419064832 | bytes 7474176 | tf_op jit(solution)/shard_map/dot_general | solution.py:24
  134.7 4.7 copy.57
  140.0 1.2 fusion.12
  142.6 13.1 %attend.1 = (bf16[2,128,768]{2,1,0:T(8,128)(2,1)}, f32[2,6,256,128]{3,2,1,0:T(8,128)}) custom-call(s32[2,128,128]{2,1,0:T(8,128)} %broadcast_in_dim.28.qid_ref, s32[2,8,1024]{2,1,0:T(8,128)} %broadcast_in_dim.29.kid_ref, bf16[2,128,768]{2,1,0:T(8,128)(2,1)} %bitcast.192, bf16[2,1024,768]{2,1,0:T(8,128)(2,1)} %bitcast.148, bf16[2,1024,768]{2,1,0:T(8,128)(2,1)} %bitcast.150), custom_call_target="tpu_custom_call" | custom-call | flops 1610612736 | bytes 6291456 | tf_op jit(solution)/shard_map/attend/pallas_call | solution.py:97
  156.2 47.6 %all-gather.8.cloned.1.call-done = bf16[32,216,768]{2,1,0:T(8,128)(2,1)} async-done(((bf16[1,216,768]{2,1,0:T(8,128)(2,1)}), bf16[32,216,768]{2,1,0:T(8,128)(2,1)}) %all-gather.8.cloned.1.call-update) | async-done | bytes 10616848 | tf_op jit(solution)/shard_map/all_gather | solution.py:218
  203.8 6.6 %fusion.36 = (bf16[32,96,768]{2,1,0:T(8,128)(2,1)}, bf16[32,96,768]{2,1,0:T(8,128)(2,1)S(1)}) fusion(bf16[32,216,768]{2,1,0:T(8,128)(2,1)} %all-gather.8.cloned.1.call-done), kind=kLoop, calls=%fused_computation.112 | loop fusion | bytes 18874368 | tf_op jit(solution)/shard_map/slice | solution.py:221
  210.4 2.3 copy.58
  212.8 1.0 copy.64
  213.8 1.4 slice.201
  216.0 8.3 %multiply_convert_fusion = (bf16[256,3072]{1,0:T(8,128)(2,1)S(1)}, f32[256,3072]{1,0:T(8,128)S(1)}, f32[256,3072]{1,0:T(8,128)S(1)}) fusion(f32[3072]{0:T(1024)S(1)} %add.142, bf16[768,3072]{1,0:T(8,128)(2,1)S(1)} %bitcast.160, f32[256,768]{1,0:T(8,128)S(1)} %get-tuple-element.70, f32[768]{0:T(1024)S(1)} %add.139, f32[768]{0:T(1024)S(1)} %mul.145, ...), kind=kOutput, calls=%fused_computation.9 | convolution fusion | flops 1260847104 | bytes 13389824 | tf_op jit(solution)/shard_map/dot_general | solution.py:24
  224.4 1.5 fusion.42
  226.2 1.7 fusion.19
  227.9 0.9 convert_reduce_fusion.3
  228.8 2.8 fusion.43
  231.6 2.2 multiply_reduce_fusion
  233.8 0.9 convert_reduce_fusion.2
  234.7 1.3 convolution_convert_fusion.4
  235.9 16.6 %attend_back.1 = (bf16[2,128,768]{2,1,0:T(8,128)(2,1)}, bf16[2,1024,768]{2,1,0:T(8,128)(2,1)}, bf16[2,1024,768]{2,1,0:T(8,128)(2,1)}) custom-call(s32[2,128,128]{2,1,0:T(8,128)} %broadcast_in_dim.28.qid_ref, s32[2,8,1024]{2,1,0:T(8,128)} %broadcast_in_dim.29.kid_ref, bf16[2,128,768]{2,1,0:T(8,128)(2,1)} %bitcast.193, bf16[2,1024,768]{2,1,0:T(8,128)(2,1)} %bitcast.149, ...), custom_call_target="tpu_custom_call" | custom-call | flops 4026531840 | bytes 12582912 | tf_op jit(solution)/shard_map/attend_back/pallas_call | solution.py:119
  252.6 4.8 fusion.44
  257.5 4.1 add_convert_fusion
  263.3 3.0 reduce.5
  267.0 1.4 reshape.439
  268.4 1.4 reshape.440
  269.7 1.4 reshape.441
  271.1 1.4 reshape.442
  272.5 1.3 reshape.443
  273.8 1.3 reshape.444
  275.2 1.4 reshape.445
  276.5 1.4 reshape.447
  277.9 1.5 concatenate.69
  279.4 0.9 pad.10
  280.9 1.2 constant_dynamic-update-slice_fusion.4
  282.1 4.7 bitcast_convert_fusion.1
  286.8 1.1 constant_dynamic-update-slice_fusion.3
  288.0 2.6 bitcast_convert_fusion
  290.6 1.1 constant_dynamic-update-slice_fusion.2
  292.2 1.2 constant_dynamic-update-slice_fusion.1
  294.3 3.1 convolution_convert_fusion.1
  297.4 2.4 constant_dynamic-update-slice_fusion.9
  299.9 1.6 convolution_convert_fusion
  301.8 1.2 constant_dynamic-update-slice_fusion.8
  303.0 1.2 constant_dynamic-update-slice_fusion.7
  304.1 1.1 constant_dynamic-update-slice_fusion.6
  305.3 1.1 constant_dynamic-update-slice_fusion.5
  306.4 2.4 fusion.9
  308.8 103.2 %reduce-scatter.6.cloned.1.call-done = bf16[1,104,768]{2,1,0:T(8,128)(2,1)} async-done(((bf16[32,104,768]{2,1,0:T(8,128)(2,1)}), bf16[1,104,768]{2,1,0:T(8,128)(2,1)}) %reduce-scatter.6.cloned.1.call-update) | async-done | bytes 159760 | tf_op jit(solution)/shard_map/reduce_scatter | solution.py:331
  413.3 0.9 convert_element_type.178
  415.6 137.6 %reduce-scatter.8.cloned.1.call-done = bf16[1,192,768]{2,1,0:T(8,128)(2,1)} async-done(((bf16[32,192,768]{2,1,0:T(8,128)(2,1)}), bf16[1,192,768]{2,1,0:T(8,128)(2,1)}) %reduce-scatter.8.cloned.1.call-update) | async-done | bytes 294928 | tf_op jit(solution)/shard_map/reduce_scatter | solution.py:283
  553.2 0.9 slice.225
  554.8 1.0 convert_element_type.181
  (131 shorter events, 21.7 us)
Async XLA Ops:
  7.2 14.5 %copy-start.24 = (s32[2,64]{1,0:T(2,128)S(1)}, s32[2,64]{1,0:T(2,128)}, u32[]{:S(2)}) copy-start(s32[2,64]{1,0:T(2,128)} %param.34) | copy-start | bytes 1540
  7.2 41.6 %all-gather.6.cloned.1.call-start = ((), (), s32[]{:S(2)}) async-start(), calls=%async_computation.4 | async-start | bytes 3538944 | tf_op jit(solution)/shard_map/all_gather | solution.py:216
  9.2 104.8 %all-gather.4.cloned.1.call-start = ((), (), s32[]{:S(2)}) async-start(), calls=%async_computation.3 | async-start | bytes 4055040 | tf_op jit(solution)/shard_map/all_gather | solution.py:217
  17.8 186.0 %all-gather.8.cloned.1.call-start = ((), (), s32[]{:S(2)}) async-start(), calls=%async_computation.5 | async-start | bytes 10948608 | tf_op jit(solution)/shard_map/all_gather | solution.py:218
  20.9 0.7 copy-start.17
  21.6 284.8 %reduce-scatter.4.cloned.1.call-start = ((), (), s32[]{:S(2)}) async-start(), calls=%async_computation.6 | async-start | bytes 3538944 | tf_op jit(solution)/shard_map/reduce_scatter | solution.py:301
  116.2 3.4 copy-start.8
  118.6 1.0 copy-start.15
  118.6 9.9 %copy-start.13 = (bf16[32,24,768]{2,1,0:T(8,128)(2,1)}, bf16[32,24,768]{2,1,0:T(8,128)(2,1)S(1)}, u32[]{:S(2)}) copy-start(bf16[32,24,768]{2,1,0:T(8,128)(2,1)S(1)} %get-tuple-element.45) | copy-start | bytes 3538948
  134.7 5.1 copy-start
  134.7 5.2 copy-start.2
  212.7 2.4 copy-start.9
  215.2 9.2 %slice-start = ((s8[4718592]{0:T(1024)(128)(4,1)}), s8[4194304]{0:T(1024)(128)(4,1)S(1)}, s32[]{:S(2)}) async-start(s8[4718592]{0:T(1024)(128)(4,1)} %bitcast.164), calls=%async_computation.9 | async-start | bytes 8388608
  215.8 18.0 %copy-start.18 = (f32[256]{0:T(256)}, f32[256]{0:T(256)S(1)}, u32[]{:S(2)}) copy-start(f32[256]{0:T(256)S(1)} %broadcast_multiply_fusion.4) | copy-start | bytes 3076
  216.0 17.8 %copy-start.20 = (f32[256]{0:T(256)}, f32[256]{0:T(256)S(1)}, u32[]{:S(2)}) copy-start(f32[256]{0:T(256)S(1)} %add_rsqrt_fusion.1) | copy-start | bytes 3076
  216.0 8.4 %slice-start.1 = ((s8[4718592]{0:T(1024)(128)(4,1)}), s8[524288]{0:T(1024)(128)(4,1)S(1)}, s32[]{:S(2)}) async-start(s8[4718592]{0:T(1024)(128)(4,1)} %bitcast.164), calls=%async_computation.10 | async-start | bytes 1048576
  216.0 8.4 %copy-start.23 = (f32[768]{0:T(1024)S(1)}, f32[768]{0:T(1024)}, u32[]{:S(2)}) copy-start(f32[768]{0:T(1024)} %add.145) | copy-start | bytes 9220
  224.4 1.6 copy-start.1
  224.4 3.5 copy-start.22
  228.8 2.8 copy-start.4
  231.6 2.2 copy-start.11
  235.9 16.6 %copy-start.16 = (bf16[32,24,768]{2,1,0:T(8,128)(2,1)S(1)}, bf16[32,24,768]{2,1,0:T(8,128)(2,1)}, u32[]{:S(2)}) copy-start(bf16[32,24,768]{2,1,0:T(8,128)(2,1)} %copy-done.15) | copy-start | bytes 3538948
  252.6 4.9 copy-start.6
  252.6 4.9 copy-start.14
  261.5 150.5 %reduce-scatter.6.cloned.1.call-start = ((), (), s32[]{:S(2)}) async-start(), calls=%async_computation.7 | async-start | bytes 5271552 | tf_op jit(solution)/shard_map/reduce_scatter | solution.py:331
  262.5 3.8 copy-start.3
  279.4 2.7 copy-start.5
  282.1 5.8 %copy-start.7 = (bf16[2,1024,768]{2,1,0:T(8,128)(2,1)S(1)}, bf16[2,1024,768]{2,1,0:T(8,128)(2,1)}, u32[]{:S(2)}) copy-start(bf16[2,1024,768]{2,1,0:T(8,128)(2,1)} %get-tuple-element.26) | copy-start | bytes 9437188
  288.0 3.8 copy-start.10
  294.3 258.9 %reduce-scatter.8.cloned.1.call-start = ((), (), s32[]{:S(2)}) async-start(), calls=%async_computation.8 | async-start | bytes 9732096 | tf_op jit(solution)/shard_map/reduce_scatter | solution.py:283
  297.4 2.5 copy-start.12
  297.4 2.5 copy-start.19
  297.4 2.4 copy-start.21
Sparse Core Ops, SparseCore 0:
  10.2 38.5 all-gather.5
  52.4 61.5 all-gather.3
  117.6 86.1 all-gather.7
  261.7 36.3 reduce-scatter.3
  303.5 108.5 reduce-scatter.5
  418.8 134.3 reduce-scatter.7
